TPU v7x, 32 devices: a whole 2x2x4 slice. The times are simulated.
32 devices in a mesh: grp: 2 (over y), wide: 4 (over z), narrow: 4 (over x, core).
Axes of the slice: x: 2, y: 2, z: 4, core: 2. Of those that a mesh axis runs over, the one named last changes fastest.
Arguments:
- moe_input: bfloat16 [4096, 7168], P(('grp', 'wide', 'narrow')), parts along dimension 0, may hold values from -6 to 6
- expert_ids: int32 [4096, 8], P(('grp', 'wide', 'narrow')), parts along dimension 0, may hold values from 0 to 255, all different within a row; in each aligned block of 128 rows (0 to 127, 128 to 255, ...) at most 8 rows name the same one
- route_weights: float32 [4096, 8], P(('grp', 'wide', 'narrow')), parts along dimension 0, may hold values from 0.1 to 1
- expert_gate: bfloat16 [7168, 2048], P('wide', 'narrow'), may hold values from -0.0625 to 0.0625
- expert_up: bfloat16 [7168, 2048], P('wide', 'narrow'), may hold values from -0.0625 to 0.0625
- expert_down: bfloat16 [2048, 7168], P(None, ('wide', 'narrow')), may hold values from -0.125 to 0.125
Outputs:
- moe_output: bfloat16 [4096, 7168], P(('grp', 'wide', 'narrow')), parts along dimension 0
There are 2 independent parts, one for each index of `grp`. A program takes and returns all parts, laid end to end along the dimension named above; an argument that names none is the same for every part. Nothing has to cross between parts.
Inputs may be any that keep to these rules, and one draw needn't show every extreme that they name: `expert_ids`: each row names 8 different experts. Among the 128 rows of one device (aligned blocks of 128 rows) no expert is named by more than 8 rows, a bound that some block reaches.
All inputs are finite; a program needn't handle non-finite values.
Results may differ from a plain program's by a relative error of at most 0.0058.
Values may be sent and summed in bfloat16 or wider, within the bound.
A program may use at most 64 MiB of HBM per device.

v0:
```python
import jax
import jax.numpy as jnp
from jax import lax
from jax.sharding import PartitionSpec as P

GROUP = 4
CAP = 8


def from_partner(block, axis, stride):
    count = lax.axis_size(axis)
    route = []
    for low in range(count):
        high = low | 1 << stride
        if high != low and high < count:
            route += [(low, high), (high, low)]
    return lax.ppermute(block, axis, route)


def shards(moe_input, expert_ids, route_weights, expert_gate, expert_up, expert_down):
    wide_count = lax.axis_size("wide")
    narrow_count = lax.axis_size("narrow")
    hosted = wide_count // GROUP
    row_count = moe_input.shape[0]
    quarter = moe_input.shape[1] // GROUP
    hidden_width = expert_gate.shape[1]
    out_cols = expert_down.shape[1]
    matches = expert_ids[:, :, None] == jnp.arange(hosted, dtype=jnp.int32)[None, None, :]
    routed = jnp.any(matches, axis=1).astype(jnp.int32)
    route_gain = jnp.sum(jnp.where(matches, route_weights[:, :, None], 0.0), axis=1)
    slot_rank = jnp.cumsum(routed, axis=0) - routed
    selector = (slot_rank.T[:, None, :] == jnp.arange(CAP, dtype=jnp.int32)[None, :, None]) & (
        routed.T[:, None, :] > 0
    )
    quarters = moe_input.reshape(row_count, GROUP, quarter)
    outgoing = jnp.einsum(
        "ecr,rqd->eqcd", selector.astype(jnp.bfloat16), quarters, preferred_element_type=jnp.float32
    )
    outgoing = outgoing.astype(jnp.bfloat16).reshape(hosted * GROUP, CAP, quarter)
    arrived = lax.all_to_all(outgoing, "wide", split_axis=0, concat_axis=1, tiled=True).reshape(
        wide_count * CAP, quarter
    )
    segment = lax.all_gather(arrived, "narrow", axis=0, tiled=True)
    gate_part = jnp.dot(segment, expert_gate, preferred_element_type=jnp.float32)
    up_part = jnp.dot(segment, expert_up, preferred_element_type=jnp.float32)
    partial_sums = jnp.concatenate([gate_part, up_part], axis=1)
    summed = partial_sums
    for level in range(2):
        summed = summed + from_partner(summed, "wide", level)
    hidden = (jax.nn.silu(summed[:, :hidden_width]) * summed[:, hidden_width:]).astype(jnp.bfloat16)
    expert_out = jnp.dot(
        lax.all_gather(hidden, "narrow", axis=1, tiled=True),
        expert_down,
        preferred_element_type=jnp.float32,
    ).astype(jnp.bfloat16)
    sectioned = expert_out.reshape(narrow_count, wide_count, CAP, 1, out_cols)
    returned = lax.all_to_all(
        lax.all_to_all(sectioned, "wide", split_axis=1, concat_axis=3, tiled=True),
        "narrow",
        split_axis=0,
        concat_axis=4,
        tiled=True,
    )
    returned = returned.reshape(CAP, hosted, GROUP * quarter)
    weighted = selector.astype(jnp.float32) * route_gain.T[:, None, :]
    combined = jnp.einsum(
        "ecr,ced->rd", weighted, returned.astype(jnp.float32), precision=lax.Precision.HIGHEST
    )
    return combined.astype(jnp.bfloat16)


def solution(mesh):
    in_specs = (
        P(("grp", "wide", "narrow"), None),
        P(("grp", "wide", "narrow"), None),
        P(("grp", "wide", "narrow"), None),
        P("wide", "narrow"),
        P("wide", "narrow"),
        P(None, ("wide", "narrow")),
    )
    out_specs = P(("grp", "wide", "narrow"), None)
    return jax.shard_map(shards, mesh=mesh, in_specs=in_specs, out_specs=out_specs, check_vma=False)
```

profile of v0, /device:TPU:0, one launch (start us, length us, event | category | flops | bytes accessed | tf_op | source)
XLA Modules:
  0.0 89.5 jit_solution(7813115647382998922)
XLA Ops:
  0.0 0.0 copy-start
  0.0 0.9 select_reduce_fusion
  0.9 0.1 copy.13
  1.0 0.2 reduce-window.7
  1.2 0.1 reduce.4
  1.3 1.8 %fusion = bf16[4,8,1792]{2,1,0:T(8,128)(2,1)S(1)} fusion(bf16[16,4,8,1792]{3,2,1,0:T(8,128)(2,1)} %bitcast.34, s32[128]{0:T(128)S(1)} %convert_subtract_fusion, pred[128]{0:T(512)(128)(4,1)S(1)} %get-tuple-element.7), kind=kOutput, calls=%fused_computation.2 | convolution fusion | flops 14739456 | bytes 1950336 | tf_op jit(solution)/shard_map/ecr,rqd->eqcd/dot_general | solution.py:36
  3.1 0.0 copy-start.1
  3.1 12.1 %all_to_all.42 = bf16[4,8,1792]{2,1,0:T(8,128)(2,1)S(1)} all-to-all(bf16[4,8,1792]{2,1,0:T(8,128)(2,1)S(1)} %fusion), channel_id=1, replica_groups=mesh['grp'=2,'wide'=4,'narrow'=4] {'wide'}, dimensions={0} | all-to-all | bytes 229376 | tf_op jit(solution)/shard_map/all_to_all | solution.py:40
  15.3 6.8 %all_gather.6 = bf16[128,1792]{1,0:T(8,128)(2,1)S(1)} all-gather(bf16[32,1792]{1,0:T(8,128)(2,1)S(1)} %bitcast.38), channel_id=1, replica_groups=mesh['grp'=2,'wide'=4,'narrow'=4] {'narrow'}, dimensions={0}, use_global_device_ids=true | all-gather | bytes 573440 | tf_op jit(solution)/shard_map/all_gather | solution.py:43
  22.1 0.0 copy-done
  22.1 0.4 fusion.18
  22.5 0.0 copy-done.1
  22.5 0.4 fusion.17
  23.0 1.2 %collective-permute-start = (f32[128,1024]{1,0:T(8,128)S(1)}, f32[128,1024]{1,0:T(8,128)S(1)}, u32[]{:S(2)}, u32[]{:S(2)}) collective-permute-start(f32[128,1024]{1,0:T(8,128)S(1)} %pad_maximum_fusion), channel_id=1, source_target_pairs={{0,4},{4,0},{8,12},{12,8},{1,5},{5,1},{9,13},{13,9},{2,6},{6,2},{1... | collective-permute-start | bytes 1572872 | tf_op jit(solution)/shard_map/ppermute | solution.py:17
  24.2 13.0 %collective-permute-done = f32[128,1024]{1,0:T(8,128)S(1)} collective-permute-done((f32[128,1024]{1,0:T(8,128)S(1)}, f32[128,1024]{1,0:T(8,128)S(1)}, u32[]{:S(2)}, u32[]{:S(2)}) %collective-permute-start) | collective-permute-done | bytes 524320 | tf_op jit(solution)/shard_map/ppermute | solution.py:17
  37.2 0.1 fusion.16
  37.3 0.0 copy-start.2
  37.3 0.9 %collective-permute-start.1 = (f32[128,1024]{1,0:T(8,128)S(1)}, f32[128,1024]{1,0:T(8,128)S(1)}, u32[]{:S(2)}, u32[]{:S(2)}) collective-permute-start(f32[128,1024]{1,0:T(8,128)S(1)} %fusion.16), channel_id=1, source_target_pairs={{0,8},{8,0},{4,12},{12,4},{1,9},{9,1},{5,13},{13,5},{2,10},{10,2},... | collective-permute-start | bytes 1572872 | tf_op jit(solution)/shard_map/ppermute | solution.py:17
  38.2 24.6 %collective-permute-done.1 = f32[128,1024]{1,0:T(8,128)S(1)} collective-permute-done((f32[128,1024]{1,0:T(8,128)S(1)}, f32[128,1024]{1,0:T(8,128)S(1)}, u32[]{:S(2)}, u32[]{:S(2)}) %collective-permute-start.1) | collective-permute-done | bytes 524320 | tf_op jit(solution)/shard_map/ppermute | solution.py:17
  62.8 0.1 add.11
  62.9 0.1 fusion.3
  63.0 6.7 %all_gather.7 = bf16[128,2048]{1,0:T(8,128)(2,1)S(1)} all-gather(bf16[128,512]{1,0:T(8,128)(2,1)S(1)} %fusion.3), channel_id=1, replica_groups=mesh['grp'=2,'wide'=4,'narrow'=4] {'narrow'}, dimensions={1}, use_global_device_ids=true | all-gather | bytes 655360 | tf_op jit(solution)/shard_map/all_gather | solution.py:52
  69.7 0.0 copy-done.2
  69.7 0.6 convolution_convert_fusion.2
  70.3 0.1 copy.15
  70.5 8.9 %all_to_all.43 = bf16[4,4,8,1,448]{4,2,0,3,1:T(8,128)(2,1)S(1)} all-to-all(bf16[4,4,8,1,448]{4,2,0,3,1:T(8,128)(2,1)S(1)} %copy.16), channel_id=1, replica_groups=mesh['grp'=2,'wide'=4,'narrow'=4] {'wide'}, dimensions={1} | all-to-all | bytes 229376 | tf_op jit(solution)/shard_map/all_to_all | solution.py:58
  79.4 7.0 %all_to_all.44 = bf16[4,1,8,4,448]{4,2,3,1,0:T(8,128)(2,1)S(1)} all-to-all(bf16[4,1,8,4,448]{4,2,3,1,0:T(8,128)(2,1)S(1)} %copy.17), channel_id=1, replica_groups=mesh['grp'=2,'wide'=4,'narrow'=4] {'narrow'}, dimensions={0} | all-to-all | bytes 229376 | tf_op jit(solution)/shard_map/all_to_all | solution.py:57
  86.4 0.1 copy.18
  86.5 0.2 reshape.145
  86.7 2.9 %convolution_convert_fusion = bf16[128,7168]{1,0:T(8,128)(2,1)} fusion(bf16[8,7168]{1,0:T(8,128)(2,1)S(1)} %reshape.145, f32[128]{0:T(128)S(1)} %get-tuple-element.5, s32[128]{0:T(128)S(1)} %convert_subtract_fusion, pred[128]{0:T(512)(128)(4,1)S(1)} %get-tuple-element.7), kind=kOutput, calls=%fused_computation | convolution fusion | flops 89000960 | bytes 1950848 | tf_op jit(solution)/shard_map/ecr,ced->rd/dot_general | solution.py:66
  (6 shorter events, 0.1 us)
Async XLA Ops:
  0.0 22.1 %copy-start = (bf16[1792,512]{1,0:T(8,128)(2,1)S(1)}, bf16[1792,512]{1,0:T(8,128)(2,1)}, u32[]{:S(2)}) copy-start(bf16[1792,512]{1,0:T(8,128)(2,1)} %param.10) | copy-start | bytes 5505028
  3.1 19.4 %copy-start.1 = (bf16[1792,512]{1,0:T(8,128)(2,1)S(1)}, bf16[1792,512]{1,0:T(8,128)(2,1)}, u32[]{:S(2)}) copy-start(bf16[1792,512]{1,0:T(8,128)(2,1)} %param.9) | copy-start | bytes 5505028
  23.0 14.2 %collective-permute-start = (f32[128,1024]{1,0:T(8,128)S(1)}, f32[128,1024]{1,0:T(8,128)S(1)}, u32[]{:S(2)}, u32[]{:S(2)}) collective-permute-start(f32[128,1024]{1,0:T(8,128)S(1)} %pad_maximum_fusion), channel_id=1, source_target_pairs={{0,4},{4,0},{8,12},{12,8},{1,5},{5,1},{9,13},{13,9},{2,6},{6,2},{1... | collective-permute-start | bytes 1572872 | tf_op jit(solution)/shard_map/ppermute | solution.py:17
  37.3 32.4 %copy-start.2 = (bf16[2048,448]{0,1:T(8,128)(2,1)S(1)}, bf16[2048,448]{0,1:T(8,128)(2,1)}, u32[]{:S(2)}) copy-start(bf16[2048,448]{0,1:T(8,128)(2,1)} %param.11) | copy-start | bytes 5505028
  37.3 25.6 %collective-permute-start.1 = (f32[128,1024]{1,0:T(8,128)S(1)}, f32[128,1024]{1,0:T(8,128)S(1)}, u32[]{:S(2)}, u32[]{:S(2)}) collective-permute-start(f32[128,1024]{1,0:T(8,128)S(1)} %fusion.16), channel_id=1, source_target_pairs={{0,8},{8,0},{4,12},{12,4},{1,9},{9,1},{5,13},{13,5},{2,10},{10,2},... | collective-permute-start | bytes 1572872 | tf_op jit(solution)/shard_map/ppermute | solution.py:17
where the time goes:
time: 89.8 us; the launch traced here: 89.5 us
  blocking collectives  41.6 us (46%)
  waiting for transfers between devices  37.7 us (42%)
  matrix products  6.15 us (7%)
  starting transfers between devices  2.14 us (2%)
  other arithmetic  1.41 us (2%)
    ppermute x2, waiting for transfers between devices, from_partner(): return lax.ppermute(block, axis, route)  37.7 us
    all_to_all x1, blocking collectives, shards(): lax.all_to_all(outgoing, 'wide', split_axis=0, concat_axis=1, tiled=True)  12.1 us
    all_to_all x1, blocking collectives, shards(): lax.all_to_all(sectioned, 'wide', split_axis=1, concat_axis=3, tiled=True)  8.89 us
    all_to_all x1, blocking collectives, shards(): lax.all_to_all(lax.all_to_all(sectioned, 'wide', split_axis=1, concat_axi...  7.02 us
    all_gather x1, blocking collectives, shards(): segment = lax.all_gather(arrived, 'narrow', axis=0, tiled=True)  6.8 us
    all_gather x1, blocking collectives, shards(): lax.all_gather(hidden, 'narrow', axis=1, tiled=True)  6.69 us
    dot_general x1, matrix products, shards(): jnp.einsum('ecr,ced->rd', weighted, returned.astype(jnp.float32), precisi...  2.86 us
    ppermute x2, starting transfers between devices, from_partner(): return lax.ppermute(block, axis, route)  2.14 us
  transfers between devices with their start and end apart: 2, of which 2 were waited for; matrix products, arithmetic and copies ran while one was open for 0% of the time, Pallas kernels for 0%

commit v1 on v0

--- a/solution.py
+++ b/solution.py
@@ -1,10 +1,290 @@
+import functools
+
 import jax
 import jax.numpy as jnp
 from jax import lax
+from jax.experimental import pallas as pl
+from jax.experimental.pallas import tpu as pltpu
 from jax.sharding import PartitionSpec as P
 
 GROUP = 4
 CAP = 8
+MESH = pl.DeviceIdType.MESH
+F32 = jnp.float32
+BF16 = jnp.bfloat16
+
+
+def slot_rows(ids):
+    rows = ids.shape[0]
+    hit = (ids == 0).astype(F32).astype(BF16)
+    ones = jnp.ones((16, ids.shape[1]), BF16)
+    routed = lax.dot_general(ones, hit, (((1,), (1,)), ((), ())), preferred_element_type=F32)
+    before = lax.broadcasted_iota(jnp.int32, (rows, rows), 0) < lax.broadcasted_iota(jnp.int32, (rows, rows), 1)
+    rank = jnp.dot(routed.astype(BF16), before.astype(F32).astype(BF16), preferred_element_type=F32)
+    slot = lax.broadcasted_iota(jnp.int32, (16, rows), 0)
+    slot = jnp.where(slot >= CAP, slot - CAP, slot).astype(F32)
+    return jnp.where((rank == slot) & (routed > 0.5), 1.0, 0.0).astype(BF16)
+
+
+def expert_kernel(
+    ids_ref, x_hbm, gate_hbm, up_hbm, down_hbm, ret_ref,
+    x_v, gu_v, down_v, xq, seg, lhs, pbuf, rs, own, hid, obuf, ret,
+    x_sem, gu_sem, down_sem,
+    a_send, a_recv, b_send, b_recv, c_send, c_recv,
+    r_send, r_recv,
+    ha_send, ha_recv, hb_send, hb_recv, hc_send, hc_recv,
+    o_send, o_recv,
+):
+    w = lax.axis_index("wide")
+    n = lax.axis_index("narrow")
+    me = w * 4 + n
+    mate = n + 1 - 2 * lax.rem(n, 2)
+    across = lax.rem(n + 2, 4)
+    diag = lax.rem(mate + 2, 4)
+    quarter = gate_hbm.shape[0]
+    half = quarter // 2
+    block = gate_hbm.shape[1] // 4
+    rows = lhs.shape[0]
+
+    def ahead(k):
+        return lax.rem(w + k, 4)
+
+    def behind(k):
+        return lax.rem(w + 4 - k, 4)
+
+    loads_x = []
+    for k in (2, 1, 3, 0):
+        cols = pl.ds(pl.multiple_of(ahead(k) * quarter, 128), quarter)
+        loads_x.append(pltpu.make_async_copy(x_hbm.at[:, cols], x_v.at[k], x_sem.at[k]))
+    for copy in loads_x:
+        copy.start()
+    loads_gu = []
+    for j in range(4):
+        for half_no, src in ((0, gate_hbm), (1, up_hbm)):
+            loads_gu.append(
+                pltpu.make_async_copy(
+                    src.at[:, pl.ds(j * block, block)],
+                    gu_v.at[:, pl.ds((2 * j + half_no) * block, block)],
+                    gu_sem.at[2 * j + half_no],
+                )
+            )
+    for copy in loads_gu:
+        copy.start()
+    load_down = pltpu.make_async_copy(down_hbm, down_v, down_sem.at[0])
+    load_down.start()
+
+    barrier = pltpu.get_barrier_semaphore()
+    for t in range(1, 16):
+        d = lax.rem(me + t, 16)
+        pl.semaphore_signal(
+            barrier, inc=1, device_id={"wide": d // 4, "narrow": lax.rem(d, 4)}, device_id_type=MESH
+        )
+
+    pick = slot_rows(ids_ref[...])
+
+    def gathered(k):
+        first = jnp.dot(pick, x_v[k, :, :half], preferred_element_type=F32)
+        second = jnp.dot(pick, x_v[k, :, half:], preferred_element_type=F32)
+        return jnp.concatenate([first[:CAP], second[CAP:]], axis=0).astype(BF16)
+
+    pl.semaphore_wait(barrier, 15)
+
+    def remote(src, dst, send, recv, device):
+        return pltpu.make_async_remote_copy(
+            src_ref=src, dst_ref=dst, send_sem=send, recv_sem=recv, device_id=device, device_id_type=MESH
+        )
+
+    started = []
+
+    def go(copy):
+        copy.start()
+        started.append(copy)
+        return copy
+
+    def spread(buf, place, a_copies, bs, br, cs, cr):
+        cross = {}
+        close = {}
+        last = {}
+
+        def forward(k):
+            s = place(behind(k), n)
+            close[k] = go(remote(buf.at[s], buf.at[s], bs.at[k], br.at[k], {"narrow": mate}))
+            cross[k] = go(remote(buf.at[s], buf.at[s], bs.at[4 + k], br.at[4 + k], {"narrow": across}))
+
+        def relay(k):
+            cross[k].wait_recv()
+            s = place(behind(k), across)
+            last[k] = go(remote(buf.at[s], buf.at[s], cs.at[k], cr.at[k], {"narrow": mate}))
+
+        forward(0)
+        order = (0, 1, 3, 2)
+        for i in range(1, 4):
+            a_copies[order[i]].wait_recv()
+            forward(order[i])
+            relay(order[i - 1])
+        relay(order[3])
+        return close, last
+
+    seg_place = lambda w_, n_: w_ * 4 + n_
+    a_copies = {}
+    for i, k in enumerate((2, 1, 3, 0)):
+        loads_x[i].wait()
+        value = gathered(k)
+        if k:
+            xq[k] = value
+            a_copies[k] = go(
+                remote(xq.at[k], seg.at[me], a_send.at[k], a_recv.at[k], {"wide": ahead(k)})
+            )
+        else:
+            seg[me] = value
+    close, last = spread(seg, seg_place, a_copies, b_send, b_recv, c_send, c_recv)
+    for k in range(4):
+        close[k].wait_recv()
+    for k in range(4):
+        last[k].wait_recv()
+    for j in range(4):
+        part = seg[4 * j:4 * j + 4].astype(F32)
+        lhs[32 * j:32 * j + 32, :half] = part[:, :CAP].reshape(32, half).astype(BF16)
+        lhs[32 * j:32 * j + 32, half:] = part[:, CAP:].reshape(32, half).astype(BF16)
+    for copy in loads_gu:
+        copy.wait()
+
+    r_copies = {}
+    for k in (2, 1, 3, 0):
+        cols = pl.ds(pl.multiple_of(ahead(k) * 2 * block, 128), 2 * block)
+        value = jnp.dot(lhs[...], gu_v[:, cols], preferred_element_type=F32)
+        if k:
+            pbuf[k] = value.astype(BF16)
+            r_copies[k] = go(remote(pbuf.at[k], rs.at[k], r_send.at[k], r_recv.at[k], {"wide": ahead(k)}))
+        else:
+            own[...] = value
+    for k in (1, 3, 2):
+        r_copies[k].wait_recv()
+    total = own[...] + rs[1].astype(F32) + rs[3].astype(F32) + rs[2].astype(F32)
+    gate, up = total[:, :block], total[:, block:]
+    mine = n * 4 + w
+    hid[mine] = (gate / (1.0 + jnp.exp(-gate)) * up).astype(BF16)
+
+    hid_place = lambda w_, n_: n_ * 4 + w_
+    h_copies = {}
+    for k in (2, 1, 3):
+        h_copies[k] = go(
+            remote(hid.at[mine], hid.at[mine], ha_send.at[k], ha_recv.at[k], {"wide": ahead(k)})
+        )
+    close, last = spread(hid, hid_place, h_copies, hb_send, hb_recv, hc_send, hc_recv)
+    load_down.wait()
+
+    def down_part(n_):
+        left = jnp.concatenate([hid[n_ * 4 + j] for j in range(4)], axis=1)
+        right = down_v[pl.ds(pl.multiple_of(n_ * 4 * block, 128), 4 * block), :]
+        return jnp.dot(left, right, preferred_element_type=F32)
+
+    out = down_part(n)
+    out = out + down_part(across)
+    for k in range(4):
+        close[k].wait_recv()
+    out = out + down_part(mate)
+    for k in range(4):
+        last[k].wait_recv()
+    out = out + down_part(diag)
+
+    width = out.shape[1]
+    wide_half = obuf.shape[2]
+    first = out[:, :wide_half].reshape(16, CAP, wide_half)
+    second = jnp.concatenate(
+        [out[:, wide_half:], jnp.zeros((rows, 2 * wide_half - width), F32)], axis=1
+    ).reshape(16, CAP, wide_half)
+    obuf[...] = jnp.concatenate([first, second], axis=1).astype(BF16)
+    o_copies = []
+    for t in range(1, 16):
+        d = lax.rem(me + t, 16)
+        o_copies.append(
+            go(
+                remote(
+                    obuf.at[d], ret.at[me], o_send.at[t], o_recv.at[t],
+                    {"wide": d // 4, "narrow": lax.rem(d, 4)},
+                )
+            )
+        )
+    ret[me] = obuf[me]
+    for copy in o_copies:
+        copy.wait_recv()
+    ret_ref[...] = ret[...]
+    for copy in started:
+        copy.wait_send()
+
+
+def combine_kernel(width, ids_ref, weights_ref, ret_ref, out_ref):
+    ids = ids_ref[...]
+    rows = ids.shape[0]
+    hit = ids == 0
+    gain = jnp.sum(jnp.where(hit, weights_ref[...], 0.0), axis=1, keepdims=True)
+    routed = jnp.sum(jnp.where(hit, 1.0, 0.0), axis=1, keepdims=True)
+    routed = jnp.broadcast_to(routed, (rows, 16))
+    after = lax.broadcasted_iota(jnp.int32, (rows, rows), 0) > lax.broadcasted_iota(jnp.int32, (rows, rows), 1)
+    rank = jnp.dot(after.astype(F32).astype(BF16), routed.astype(BF16), preferred_element_type=F32)
+    slot = lax.broadcasted_iota(jnp.int32, (rows, 16), 1).astype(F32)
+    place = jnp.where((rank == slot) & (routed > 0.5) & (slot < CAP), 1.0, 0.0).astype(BF16)
+    pieces = []
+    wide_half = ret_ref.shape[2]
+    for j in range(ret_ref.shape[0]):
+        value = ret_ref[j].astype(F32)
+        pieces += [value[:CAP], value[CAP:, :width - wide_half]]
+    slots = jnp.concatenate(pieces, axis=1)
+    slots = jnp.concatenate([slots, jnp.zeros_like(slots)], axis=0).astype(BF16)
+    out_ref[...] = (jnp.dot(place, slots, preferred_element_type=F32) * gain).astype(BF16)
+
+
+def grouped(moe_input, expert_ids, route_weights, expert_gate, expert_up, expert_down):
+    rows, model = moe_input.shape
+    quarter, hidden = expert_gate.shape
+    width = expert_down.shape[1]
+    block = hidden // 4
+    wide_half = -(-width // 256) * 128
+    all_rows = 16 * CAP
+    dma = pltpu.SemaphoreType.DMA
+    any_spec = pl.BlockSpec(memory_space=pl.ANY)
+    vmem_spec = pl.BlockSpec(memory_space=pltpu.VMEM)
+    returned = pl.pallas_call(
+        expert_kernel,
+        out_shape=jax.ShapeDtypeStruct((16, 16, wide_half), BF16),
+        in_specs=[vmem_spec] + [any_spec] * 4,
+        out_specs=vmem_spec,
+        scratch_shapes=[
+            pltpu.VMEM((4, rows, quarter), BF16),
+            pltpu.VMEM((quarter, 2 * hidden), BF16),
+            pltpu.VMEM(expert_down.shape, BF16),
+            pltpu.VMEM((4, 16, quarter // 2), BF16),
+            pltpu.VMEM((16, 16, quarter // 2), BF16),
+            pltpu.VMEM((all_rows, quarter), BF16),
+            pltpu.VMEM((4, all_rows, 2 * block), BF16),
+            pltpu.VMEM((4, all_rows, 2 * block), BF16),
+            pltpu.VMEM((all_rows, 2 * block), F32),
+            pltpu.VMEM((16, all_rows, block), BF16),
+            pltpu.VMEM((16, 16, wide_half), BF16),
+            pltpu.VMEM((16, 16, wide_half), BF16),
+            dma((4,)), dma((8,)), dma((1,)),
+            dma((4,)), dma((4,)), dma((8,)), dma((8,)), dma((4,)), dma((4,)),
+            dma((4,)), dma((4,)),
+            dma((4,)), dma((4,)), dma((8,)), dma((8,)), dma((4,)), dma((4,)),
+            dma((16,)), dma((16,)),
+        ],
+        compiler_params=pltpu.CompilerParams(
+            collective_id=0, has_side_effects=True, vmem_limit_bytes=56 * 1024 * 1024
+        ),
+    )(expert_ids, moe_input, expert_gate, expert_up, expert_down)
+    parts = 4
+    return pl.pallas_call(
+        functools.partial(combine_kernel, width),
+        out_shape=jax.ShapeDtypeStruct((rows, model), BF16),
+        grid=(parts,),
+        in_specs=[
+            pl.BlockSpec(expert_ids.shape, lambda i: (0, 0)),
+            pl.BlockSpec(route_weights.shape, lambda i: (0, 0)),
+            pl.BlockSpec((16 // parts, 16, wide_half), lambda i: (i, 0, 0)),
+        ],
+        out_specs=pl.BlockSpec((rows, model // parts), lambda i: (0, i)),
+    )(expert_ids, route_weights, returned)
 
 
 def from_partner(block, axis, stride):
@@ -79,4 +359,6 @@
         P(None, ("wide", "narrow")),
     )
     out_specs = P(("grp", "wide", "narrow"), None)
-    return jax.shard_map(shards, mesh=mesh, in_specs=in_specs, out_specs=out_specs, check_vma=False)
+    single = mesh.shape["wide"] == GROUP and mesh.shape["narrow"] == 4
+    per_device = grouped if single else shards
+    return jax.shard_map(per_device, mesh=mesh, in_specs=in_specs, out_specs=out_specs, check_vma=False)

time: 89.8 us -> 52.1 us (0.58)
  Pallas kernels: 0 us -> 45.7 us
  blocking collectives: 41.6 us -> 0 us
  waiting for transfers between devices: 37.7 us -> 0 us
  matrix products: 6.15 us -> 0 us
  local copies, waits for them, and re-layouts: 0.53 us -> 5.95 us
  starting transfers between devices: 2.14 us -> 0 us
  other arithmetic: 1.41 us -> 0 us
    pallas_call x0 -> x2, Pallas kernels: none -> 45.7 us  [the longest x1 41.5 us: grouped(): pl.pallas_call(expert_kernel, out_shape=jax.ShapeDtypeStruct((16, 16, wid...]
    ppermute x2 -> x0, waiting for transfers between devices: 37.7 us -> none  [from_partner(): return lax.ppermute(block, axis, route)]
    all_to_all x3 -> x0, blocking collectives: 28.1 us -> none  [the longest x1 12.1 us: shards(): lax.all_to_all(outgoing, 'wide', split_axis=0, concat_axis=1, tiled=True)]
    all_gather x2 -> x0, blocking collectives: 13.5 us -> none  [the longest x1 6.8 us: shards(): segment = lax.all_gather(arrived, 'narrow', axis=0, tiled=True)]
    dot_general x5 -> x0, matrix products: 6.15 us -> none  [the longest x1 2.86 us: shards(): jnp.einsum('ecr,ced->rd', weighted, returned.astype(jnp.float32), precisi...]
    unnamed x6 -> x5, local copies, waits for them, and re-layouts: 0.01 us -> 5.95 us
    ppermute x2 -> x0, starting transfers between devices: 2.14 us -> none  [from_partner(): return lax.ppermute(block, axis, route)]
  transfers between devices with their start and end apart: 2 -> 0, of which waited for: 2 -> 0; matrix products, arithmetic and copies ran while one was open for 0% -> 0% of each run, Pallas kernels for 0% -> 0%
where the time goes in v1:
time: 52.1 us; the launch traced here: 51.6 us
  Pallas kernels  45.7 us (88%)
  local copies, waits for them, and re-layouts  5.95 us (11%)
    pallas_call x1, Pallas kernels, grouped(): pl.pallas_call(expert_kernel, out_shape=jax.ShapeDtypeStruct((16, 16, wid...  41.5 us
    unnamed x5, local copies, waits for them, and re-layouts  5.95 us
    pallas_call x1, Pallas kernels, grouped(): pl.pallas_call(functools.partial(combine_kernel, width), out_shape=jax.Sh...  4.15 us

profile of v1, /device:TPU:0, one launch (start us, length us, event | category | flops | bytes accessed | tf_op | source)
XLA Modules:
  0.0 51.6 jit_solution(4078609980669424047)
XLA Ops:
  0.0 1.4 %copy.9.ids_ref = s32[128,8]{1,0:T(8,128)} copy(s32[128,8]{0,1:T(8,128)} %param.7) | data formatting | bytes 8192 | tf_op args[1]
  1.4 3.8 %copy.8.down_hbm = bf16[2048,448]{1,0:T(8,128)(2,1)} copy(bf16[2048,448]{0,1:T(8,128)(2,1)} %param.11) | data formatting | bytes 3670016 | tf_op args[5]
  5.2 0.0 copy-start
  5.2 41.5 %shard_map.64.ret_ref = bf16[16,16,256]{2,1,0:T(8,128)(2,1)} custom-call(s32[128,8]{1,0:T(8,128)} %copy.9.ids_ref, bf16[128,7168]{1,0:T(8,128)(2,1)} %x_hbm.1, bf16[1792,512]{1,0:T(8,128)(2,1)} %gate_hbm.1, bf16[1792,512]{1,0:T(8,128)(2,1)} %up_hbm.1, bf16[2048,448]{1,0:T(8,128)(2,1)} %copy.8.down_hbm), custom_call_target="tpu_custom_call" | custom-call | tf_op jit(solution)/shard_map/pallas_call | solution.py:248
  46.8 0.0 copy-done
  46.8 0.7 %copy.10.weights_ref = f32[128,8]{1,0:T(8,128)} copy(f32[128,8]{0,1:T(8,128)S(1)} %copy-done) | data formatting | bytes 8192 | tf_op args[2]
  47.5 4.1 %shard_map.65 = bf16[128,7168]{1,0:T(8,128)(2,1)} custom-call(s32[128,8]{1,0:T(8,128)} %copy.9.ids_ref, f32[128,8]{1,0:T(8,128)} %copy.10.weights_ref, bf16[16,16,256]{2,1,0:T(8,128)(2,1)} %shard_map.64.ret_ref), custom_call_target="tpu_custom_call" | custom-call | tf_op jit(solution)/shard_map/pallas_call | solution.py:277
Async XLA Ops:
  5.2 41.5 %copy-start = (f32[128,8]{0,1:T(8,128)S(1)}, f32[128,8]{0,1:T(8,128)}, u32[]{:S(2)}) copy-start(f32[128,8]{0,1:T(8,128)} %param.8) | copy-start | bytes 12292

commit v2 on v1

--- a/solution.py
+++ b/solution.py
@@ -15,10 +15,9 @@
 
 
 def slot_rows(ids):
-    rows = ids.shape[0]
-    hit = (ids == 0).astype(F32).astype(BF16)
-    ones = jnp.ones((16, ids.shape[1]), BF16)
-    routed = lax.dot_general(ones, hit, (((1,), (1,)), ((), ())), preferred_element_type=F32)
+    rows = ids.shape[1]
+    routed = jnp.sum(jnp.where(ids == 0, 1.0, 0.0), axis=0, keepdims=True)
+    routed = jnp.broadcast_to(routed, (16, rows))
     before = lax.broadcasted_iota(jnp.int32, (rows, rows), 0) < lax.broadcasted_iota(jnp.int32, (rows, rows), 1)
     rank = jnp.dot(routed.astype(BF16), before.astype(F32).astype(BF16), preferred_element_type=F32)
     slot = lax.broadcasted_iota(jnp.int32, (16, rows), 0)
@@ -176,8 +175,8 @@
 
     def down_part(n_):
         left = jnp.concatenate([hid[n_ * 4 + j] for j in range(4)], axis=1)
-        right = down_v[pl.ds(pl.multiple_of(n_ * 4 * block, 128), 4 * block), :]
-        return jnp.dot(left, right, preferred_element_type=F32)
+        right = down_v[:, pl.ds(pl.multiple_of(n_ * 4 * block, 128), 4 * block)]
+        return lax.dot_general(left, right, (((1,), (1,)), ((), ())), preferred_element_type=F32)
 
     out = down_part(n)
     out = out + down_part(across)
@@ -216,15 +215,12 @@
 
 def combine_kernel(width, ids_ref, weights_ref, ret_ref, out_ref):
     ids = ids_ref[...]
-    rows = ids.shape[0]
+    rows = ids.shape[1]
     hit = ids == 0
-    gain = jnp.sum(jnp.where(hit, weights_ref[...], 0.0), axis=1, keepdims=True)
-    routed = jnp.sum(jnp.where(hit, 1.0, 0.0), axis=1, keepdims=True)
-    routed = jnp.broadcast_to(routed, (rows, 16))
-    after = lax.broadcasted_iota(jnp.int32, (rows, rows), 0) > lax.broadcasted_iota(jnp.int32, (rows, rows), 1)
-    rank = jnp.dot(after.astype(F32).astype(BF16), routed.astype(BF16), preferred_element_type=F32)
-    slot = lax.broadcasted_iota(jnp.int32, (rows, 16), 1).astype(F32)
-    place = jnp.where((rank == slot) & (routed > 0.5) & (slot < CAP), 1.0, 0.0).astype(BF16)
+    gain = jnp.sum(jnp.where(hit, weights_ref[...], 0.0), axis=0, keepdims=True)
+    gain = jnp.transpose(jnp.broadcast_to(gain, (128, rows)))
+    place = slot_rows(ids)
+    place = jnp.where(lax.broadcasted_iota(jnp.int32, place.shape, 0) < CAP, place.astype(F32), 0.0).astype(BF16)
     pieces = []
     wide_half = ret_ref.shape[2]
     for j in range(ret_ref.shape[0]):
@@ -232,7 +228,9 @@
         pieces += [value[:CAP], value[CAP:, :width - wide_half]]
     slots = jnp.concatenate(pieces, axis=1)
     slots = jnp.concatenate([slots, jnp.zeros_like(slots)], axis=0).astype(BF16)
-    out_ref[...] = (jnp.dot(place, slots, preferred_element_type=F32) * gain).astype(BF16)
+    placed = lax.dot_general(place, slots, (((0,), (0,)), ((), ())), preferred_element_type=F32)
+    gains = jnp.concatenate([gain] * (placed.shape[1] // 128), axis=1)
+    out_ref[...] = (placed * gains).astype(BF16)
 
 
 def grouped(moe_input, expert_ids, route_weights, expert_gate, expert_up, expert_down):
@@ -242,6 +240,7 @@
     block = hidden // 4
     wide_half = -(-width // 256) * 128
     all_rows = 16 * CAP
+    ids, weights = expert_ids.T, route_weights.T
     dma = pltpu.SemaphoreType.DMA
     any_spec = pl.BlockSpec(memory_space=pl.ANY)
     vmem_spec = pl.BlockSpec(memory_space=pltpu.VMEM)
@@ -253,7 +252,7 @@
         scratch_shapes=[
             pltpu.VMEM((4, rows, quarter), BF16),
             pltpu.VMEM((quarter, 2 * hidden), BF16),
-            pltpu.VMEM(expert_down.shape, BF16),
+            pltpu.VMEM(expert_down.shape[::-1], BF16),
             pltpu.VMEM((4, 16, quarter // 2), BF16),
             pltpu.VMEM((16, 16, quarter // 2), BF16),
             pltpu.VMEM((all_rows, quarter), BF16),
@@ -272,19 +271,19 @@
         compiler_params=pltpu.CompilerParams(
             collective_id=0, has_side_effects=True, vmem_limit_bytes=56 * 1024 * 1024
         ),
-    )(expert_ids, moe_input, expert_gate, expert_up, expert_down)
+    )(ids, moe_input, expert_gate, expert_up, expert_down.T)
     parts = 4
     return pl.pallas_call(
         functools.partial(combine_kernel, width),
         out_shape=jax.ShapeDtypeStruct((rows, model), BF16),
         grid=(parts,),
         in_specs=[
-            pl.BlockSpec(expert_ids.shape, lambda i: (0, 0)),
-            pl.BlockSpec(route_weights.shape, lambda i: (0, 0)),
+            pl.BlockSpec(ids.shape, lambda i: (0, 0)),
+            pl.BlockSpec(weights.shape, lambda i: (0, 0)),
             pl.BlockSpec((16 // parts, 16, wide_half), lambda i: (i, 0, 0)),
         ],
         out_specs=pl.BlockSpec((rows, model // parts), lambda i: (0, i)),
-    )(expert_ids, route_weights, returned)
+    )(ids, weights, returned)
 
 
 def from_partner(block, axis, stride):

time: 52.1 us -> 45.9 us (0.88)
  local copies, waits for them, and re-layouts: 5.95 us -> 0 us
    unnamed x5 -> x0, local copies, waits for them, and re-layouts: 5.95 us -> none
where the time goes in v2:
time: 45.9 us; the launch traced here: 45.5 us
  Pallas kernels  45.5 us (99%)
    pallas_call x1, Pallas kernels, grouped(): pl.pallas_call(expert_kernel, out_shape=jax.ShapeDtypeStruct((16, 16, wid...  41.6 us
    pallas_call x1, Pallas kernels, grouped(): pl.pallas_call(functools.partial(combine_kernel, width), out_shape=jax.Sh...  3.96 us

profile of v2, /device:TPU:0, one launch (start us, length us, event | category | flops | bytes accessed | tf_op | source)
XLA Modules:
  0.0 45.5 jit_solution(5485006259100299657)
XLA Ops:
  0.0 41.6 %shard_map.64.ret_ref = bf16[16,16,256]{2,1,0:T(8,128)(2,1)} custom-call(s32[8,128]{1,0:T(8,128)} %bitcast.4, bf16[128,7168]{1,0:T(8,128)(2,1)} %x_hbm.1, bf16[1792,512]{1,0:T(8,128)(2,1)} %gate_hbm.1, bf16[1792,512]{1,0:T(8,128)(2,1)} %up_hbm.1, bf16[448,2048]{1,0:T(8,128)(2,1)} %bitcast.3), custom_call_target="tpu_custom_call" | custom-call | tf_op jit(solution)/shard_map/pallas_call | solution.py:247
  41.6 4.0 %shard_map.65 = bf16[128,7168]{1,0:T(8,128)(2,1)} custom-call(s32[8,128]{1,0:T(8,128)} %bitcast.5, f32[8,128]{1,0:T(8,128)} %bitcast.6, bf16[16,16,256]{2,1,0:T(8,128)(2,1)} %shard_map.64.ret_ref), custom_call_target="tpu_custom_call" | custom-call | tf_op jit(solution)/shard_map/pallas_call | solution.py:276

commit v3 on v2

--- a/solution.py
+++ b/solution.py
@@ -26,9 +26,9 @@
 
 
 def expert_kernel(
-    ids_ref, x_hbm, gate_hbm, up_hbm, down_hbm, ret_ref,
-    x_v, gu_v, down_v, xq, seg, lhs, pbuf, rs, own, hid, obuf, ret,
-    x_sem, gu_sem, down_sem,
+    ids_hbm, x_hbm, gate_hbm, up_hbm, down_hbm, ret_ref,
+    x_v, gu_v, down_v, xq, seg, lhs, pbuf, rs, own, hid, obuf, ret, ids_v,
+    ids_sem, x_sem, gu_sem, down_sem,
     a_send, a_recv, b_send, b_recv, c_send, c_recv,
     r_send, r_recv,
     ha_send, ha_recv, hb_send, hb_recv, hc_send, hc_recv,
@@ -51,6 +51,12 @@
     def behind(k):
         return lax.rem(w + 4 - k, 4)
 
+    barrier = pltpu.get_barrier_semaphore()
+    for device in [{"wide": ahead(k)} for k in (2, 1, 3)] + [{"narrow": across}, {"narrow": mate}]:
+        pl.semaphore_signal(barrier, inc=1, device_id=device, device_id_type=MESH)
+
+    load_ids = pltpu.make_async_copy(ids_hbm, ids_v, ids_sem.at[0])
+    load_ids.start()
     loads_x = []
     for k in (2, 1, 3, 0):
         cols = pl.ds(pl.multiple_of(ahead(k) * quarter, 128), quarter)
@@ -72,21 +78,15 @@
     load_down = pltpu.make_async_copy(down_hbm, down_v, down_sem.at[0])
     load_down.start()
 
-    barrier = pltpu.get_barrier_semaphore()
-    for t in range(1, 16):
-        d = lax.rem(me + t, 16)
-        pl.semaphore_signal(
-            barrier, inc=1, device_id={"wide": d // 4, "narrow": lax.rem(d, 4)}, device_id_type=MESH
-        )
-
-    pick = slot_rows(ids_ref[...])
+    load_ids.wait()
+    pick = slot_rows(ids_v[...])
 
     def gathered(k):
         first = jnp.dot(pick, x_v[k, :, :half], preferred_element_type=F32)
         second = jnp.dot(pick, x_v[k, :, half:], preferred_element_type=F32)
         return jnp.concatenate([first[:CAP], second[CAP:]], axis=0).astype(BF16)
 
-    pl.semaphore_wait(barrier, 15)
+    pl.semaphore_wait(barrier, 5)
 
     def remote(src, dst, send, recv, device):
         return pltpu.make_async_remote_copy(
@@ -247,7 +247,7 @@
     returned = pl.pallas_call(
         expert_kernel,
         out_shape=jax.ShapeDtypeStruct((16, 16, wide_half), BF16),
-        in_specs=[vmem_spec] + [any_spec] * 4,
+        in_specs=[any_spec] * 5,
         out_specs=vmem_spec,
         scratch_shapes=[
             pltpu.VMEM((4, rows, quarter), BF16),
@@ -262,7 +262,8 @@
             pltpu.VMEM((16, all_rows, block), BF16),
             pltpu.VMEM((16, 16, wide_half), BF16),
             pltpu.VMEM((16, 16, wide_half), BF16),
-            dma((4,)), dma((8,)), dma((1,)),
+            pltpu.VMEM(ids.shape, jnp.int32),
+            dma((1,)), dma((4,)), dma((8,)), dma((1,)),
             dma((4,)), dma((4,)), dma((8,)), dma((8,)), dma((4,)), dma((4,)),
             dma((4,)), dma((4,)),
             dma((4,)), dma((4,)), dma((8,)), dma((8,)), dma((4,)), dma((4,)),
@@ -272,7 +273,7 @@
             collective_id=0, has_side_effects=True, vmem_limit_bytes=56 * 1024 * 1024
         ),
     )(ids, moe_input, expert_gate, expert_up, expert_down.T)
-    parts = 4
+    parts = 1
     return pl.pallas_call(
         functools.partial(combine_kernel, width),
         out_shape=jax.ShapeDtypeStruct((rows, model), BF16),

time: 45.9 us -> 43.4 us (0.946)
  Pallas kernels: 45.5 us -> 43.2 us
    pallas_call x1, Pallas kernels: 41.6 us -> 40.3 us  [grouped(): pl.pallas_call(expert_kernel, out_shape=jax.ShapeDtypeStruct((16, 16, wid...]
    pallas_call x1, Pallas kernels: 3.96 us -> 2.97 us  [grouped(): pl.pallas_call(functools.partial(combine_kernel, width), out_shape=jax.Sh...]
where the time goes in v3:
time: 43.4 us; the launch traced here: 43.2 us
  Pallas kernels  43.2 us (100%)
    pallas_call x1, Pallas kernels, grouped(): pl.pallas_call(expert_kernel, out_shape=jax.ShapeDtypeStruct((16, 16, wid...  40.3 us
    pallas_call x1, Pallas kernels, grouped(): pl.pallas_call(functools.partial(combine_kernel, width), out_shape=jax.Sh...  2.97 us

profile of v3, /device:TPU:0, one launch (start us, length us, event | category | flops | bytes accessed | tf_op | source)
XLA Modules:
  0.0 43.2 jit_solution(501337236713179563)
XLA Ops:
  0.0 40.3 %shard_map.64.ret_ref = bf16[16,16,256]{2,1,0:T(8,128)(2,1)} custom-call(s32[8,128]{1,0:T(8,128)} %bitcast.4, bf16[128,7168]{1,0:T(8,128)(2,1)} %x_hbm.1, bf16[1792,512]{1,0:T(8,128)(2,1)} %gate_hbm.1, bf16[1792,512]{1,0:T(8,128)(2,1)} %up_hbm.1, bf16[448,2048]{1,0:T(8,128)(2,1)} %bitcast.3), custom_call_target="tpu_custom_call" | custom-call | tf_op jit(solution)/shard_map/pallas_call | solution.py:247
  40.3 3.0 %shard_map.65 = bf16[128,7168]{1,0:T(8,128)(2,1)} custom-call(s32[8,128]{1,0:T(8,128)} %bitcast.5, f32[8,128]{1,0:T(8,128)} %bitcast.6, bf16[16,16,256]{2,1,0:T(8,128)(2,1)} %shard_map.64.ret_ref), custom_call_target="tpu_custom_call" | custom-call | tf_op jit(solution)/shard_map/pallas_call | solution.py:277

commit v4 on v3

--- a/solution.py
+++ b/solution.py
@@ -43,7 +43,7 @@
     quarter = gate_hbm.shape[0]
     half = quarter // 2
     block = gate_hbm.shape[1] // 4
-    rows = lhs.shape[0]
+    rows = 2 * lhs.shape[1]
 
     def ahead(k):
         return lax.rem(w + k, 4)
@@ -100,31 +100,38 @@
         started.append(copy)
         return copy
 
-    def spread(buf, place, a_copies, bs, br, cs, cr):
-        cross = {}
-        close = {}
-        last = {}
-
-        def forward(k):
-            s = place(behind(k), n)
-            close[k] = go(remote(buf.at[s], buf.at[s], bs.at[k], br.at[k], {"narrow": mate}))
-            cross[k] = go(remote(buf.at[s], buf.at[s], bs.at[4 + k], br.at[4 + k], {"narrow": across}))
-
-        def relay(k):
-            cross[k].wait_recv()
-            s = place(behind(k), across)
-            last[k] = go(remote(buf.at[s], buf.at[s], cs.at[k], cr.at[k], {"narrow": mate}))
-
-        forward(0)
-        order = (0, 1, 3, 2)
-        for i in range(1, 4):
-            a_copies[order[i]].wait_recv()
-            forward(order[i])
-            relay(order[i - 1])
-        relay(order[3])
-        return close, last
-
-    seg_place = lambda w_, n_: w_ * 4 + n_
+    class Spread:
+        def __init__(self, buf, place, bs, br, cs, cr, base):
+            self.buf, self.place, self.base = buf, place, base
+            self.sems = bs, br, cs, cr
+            self.cross, self.close, self.last = {}, {}, {}
+
+        def forward(self, k):
+            bs, br, _, _ = self.sems
+            block_ref = self.buf.at[self.place(behind(k), n)]
+            i = self.base + k
+            self.cross[k] = go(remote(block_ref, block_ref, bs.at[2 * i], br.at[2 * i], {"narrow": across}))
+            self.close[k] = go(remote(block_ref, block_ref, bs.at[2 * i + 1], br.at[2 * i + 1], {"narrow": mate}))
+
+        def relay(self, k):
+            _, _, cs, cr = self.sems
+            self.cross[k].wait_recv()
+            block_ref = self.buf.at[self.place(behind(k), across)]
+            i = self.base + k
+            self.last[k] = go(remote(block_ref, block_ref, cs.at[i], cr.at[i], {"narrow": mate}))
+
+        def wait_close(self):
+            for k in self.close:
+                self.close[k].wait_recv()
+
+        def wait_last(self):
+            for k in self.last:
+                self.last[k].wait_recv()
+
+    def seg_place(w_, n_):
+        return (n_ // 2) * 8 + w_ * 2 + lax.rem(n_, 2)
+
+    seg_mine = seg_place(w, n)
     a_copies = {}
     for i, k in enumerate((2, 1, 3, 0)):
         loads_x[i].wait()
@@ -132,59 +139,116 @@
         if k:
             xq[k] = value
             a_copies[k] = go(
-                remote(xq.at[k], seg.at[me], a_send.at[k], a_recv.at[k], {"wide": ahead(k)})
+                remote(xq.at[k], seg.at[seg_mine], a_send.at[k], a_recv.at[k], {"wide": ahead(k)})
             )
         else:
-            seg[me] = value
-    close, last = spread(seg, seg_place, a_copies, b_send, b_recv, c_send, c_recv)
-    for k in range(4):
-        close[k].wait_recv()
-    for k in range(4):
-        last[k].wait_recv()
-    for j in range(4):
-        part = seg[4 * j:4 * j + 4].astype(F32)
-        lhs[32 * j:32 * j + 32, :half] = part[:, :CAP].reshape(32, half).astype(BF16)
-        lhs[32 * j:32 * j + 32, half:] = part[:, CAP:].reshape(32, half).astype(BF16)
+            seg[seg_mine] = value
+    spread = Spread(seg, seg_place, b_send, b_recv, c_send, c_recv, 0)
+    spread.forward(0)
+    a_copies[1].wait_recv()
+    spread.forward(1)
+    spread.relay(0)
+    a_copies[3].wait_recv()
+    spread.forward(3)
+    spread.relay(1)
+    a_copies[2].wait_recv()
+    spread.forward(2)
+    spread.relay(3)
+    spread.wait_close()
+
+    side = n // 2
+    part_rows = rows // 2
+
+    def fill(c):
+        part_side = side if c == 0 else 1 - side
+        part = seg[pl.ds(part_side * 8, 8)].astype(F32)
+        lhs[c, :, :half] = part[:, :CAP].reshape(part_rows, half).astype(BF16)
+        lhs[c, :, half:] = part[:, CAP:].reshape(part_rows, half).astype(BF16)
+
+    r_copies = {}
+
+    def partial_sums(c, k):
+        cols = pl.ds(pl.multiple_of(ahead(k) * 2 * block, 128), 2 * block)
+        value = jnp.dot(lhs[c], gu_v[:, cols], preferred_element_type=F32)
+        if k:
+            i = 4 * c + k
+            pbuf[i] = value.astype(BF16)
+            r_copies[i] = go(remote(pbuf.at[i], rs.at[i], r_send.at[i], r_recv.at[i], {"wide": ahead(k)}))
+        else:
+            own[c] = value
+
+    fill(0)
     for copy in loads_gu:
         copy.wait()
-
-    r_copies = {}
+    partial_sums(0, 2)
+    partial_sums(0, 1)
+    partial_sums(0, 3)
+    spread.relay(2)
+    partial_sums(0, 0)
+    spread.wait_last()
+    fill(1)
     for k in (2, 1, 3, 0):
-        cols = pl.ds(pl.multiple_of(ahead(k) * 2 * block, 128), 2 * block)
-        value = jnp.dot(lhs[...], gu_v[:, cols], preferred_element_type=F32)
-        if k:
-            pbuf[k] = value.astype(BF16)
-            r_copies[k] = go(remote(pbuf.at[k], rs.at[k], r_send.at[k], r_recv.at[k], {"wide": ahead(k)}))
-        else:
-            own[...] = value
-    for k in (1, 3, 2):
-        r_copies[k].wait_recv()
-    total = own[...] + rs[1].astype(F32) + rs[3].astype(F32) + rs[2].astype(F32)
-    gate, up = total[:, :block], total[:, block:]
-    mine = n * 4 + w
-    hid[mine] = (gate / (1.0 + jnp.exp(-gate)) * up).astype(BF16)
-
-    hid_place = lambda w_, n_: n_ * 4 + w_
+        partial_sums(1, k)
+
     h_copies = {}
-    for k in (2, 1, 3):
-        h_copies[k] = go(
-            remote(hid.at[mine], hid.at[mine], ha_send.at[k], ha_recv.at[k], {"wide": ahead(k)})
+    h_spread = {}
+
+    def hid_place(c):
+        def place(w_, n_):
+            n_side = n_ // 2
+            return (n_side if c == 0 else 1 - n_side) * 16 + n_ * 4 + w_
+
+        return place
+
+    for c in range(2):
+        for k in (1, 3, 2):
+            r_copies[4 * c + k].wait_recv()
+        total = own[c]
+        for k in (1, 3, 2):
+            total = total + rs[4 * c + k].astype(F32)
+        gate, up = total[:, :block], total[:, block:]
+        place = hid_place(c)
+        mine = place(w, n)
+        hid[mine] = (gate / (1.0 + jnp.exp(-gate)) * up).astype(BF16)
+        for k in (2, 1, 3):
+            i = 4 * c + k
+            h_copies[i] = go(
+                remote(hid.at[mine], hid.at[mine], ha_send.at[i], ha_recv.at[i], {"wide": ahead(k)})
+            )
+        h_spread[c] = Spread(hid, place, hb_send, hb_recv, hc_send, hc_recv, 4 * c)
+        h_spread[c].forward(0)
+    late = []
+    for c in range(2):
+        for done, k in ((0, 1), (1, 3), (3, 2)):
+            h_copies[4 * c + k].wait_recv()
+            h_spread[c].forward(k)
+            late.append((c, done))
+            if len(late) > 1:
+                before_c, before_k = late.pop(0)
+                h_spread[before_c].relay(before_k)
+        late.append((c, 2))
+    for before_c, before_k in late:
+        h_spread[before_c].relay(before_k)
+    load_down.wait()
+
+    def down_part(n_):
+        left = jnp.concatenate(
+            [
+                jnp.concatenate([hid[16 * s + n_ * 4 + j] for j in range(4)], axis=1)
+                for s in range(2)
+            ],
+            axis=0,
         )
-    close, last = spread(hid, hid_place, h_copies, hb_send, hb_recv, hc_send, hc_recv)
-    load_down.wait()
-
-    def down_part(n_):
-        left = jnp.concatenate([hid[n_ * 4 + j] for j in range(4)], axis=1)
         right = down_v[:, pl.ds(pl.multiple_of(n_ * 4 * block, 128), 4 * block)]
         return lax.dot_general(left, right, (((1,), (1,)), ((), ())), preferred_element_type=F32)
 
     out = down_part(n)
     out = out + down_part(across)
-    for k in range(4):
-        close[k].wait_recv()
+    for c in range(2):
+        h_spread[c].wait_close()
     out = out + down_part(mate)
-    for k in range(4):
-        last[k].wait_recv()
+    for c in range(2):
+        h_spread[c].wait_last()
     out = out + down_part(diag)
 
     width = out.shape[1]
@@ -200,12 +264,12 @@
         o_copies.append(
             go(
                 remote(
-                    obuf.at[d], ret.at[me], o_send.at[t], o_recv.at[t],
+                    obuf.at[seg_place(d // 4, lax.rem(d, 4))], ret.at[me], o_send.at[t], o_recv.at[t],
                     {"wide": d // 4, "narrow": lax.rem(d, 4)},
                 )
             )
         )
-    ret[me] = obuf[me]
+    ret[me] = obuf[seg_mine]
     for copy in o_copies:
         copy.wait_recv()
     ret_ref[...] = ret[...]
@@ -239,7 +303,7 @@
     width = expert_down.shape[1]
     block = hidden // 4
     wide_half = -(-width // 256) * 128
-    all_rows = 16 * CAP
+    part_rows = 8 * CAP
     ids, weights = expert_ids.T, route_weights.T
     dma = pltpu.SemaphoreType.DMA
     any_spec = pl.BlockSpec(memory_space=pl.ANY)
@@ -255,18 +319,18 @@
             pltpu.VMEM(expert_down.shape[::-1], BF16),
             pltpu.VMEM((4, 16, quarter // 2), BF16),
             pltpu.VMEM((16, 16, quarter // 2), BF16),
-            pltpu.VMEM((all_rows, quarter), BF16),
-            pltpu.VMEM((4, all_rows, 2 * block), BF16),
-            pltpu.VMEM((4, all_rows, 2 * block), BF16),
-            pltpu.VMEM((all_rows, 2 * block), F32),
-            pltpu.VMEM((16, all_rows, block), BF16),
+            pltpu.VMEM((2, part_rows, quarter), BF16),
+            pltpu.VMEM((8, part_rows, 2 * block), BF16),
+            pltpu.VMEM((8, part_rows, 2 * block), BF16),
+            pltpu.VMEM((2, part_rows, 2 * block), F32),
+            pltpu.VMEM((32, part_rows, block), BF16),
             pltpu.VMEM((16, 16, wide_half), BF16),
             pltpu.VMEM((16, 16, wide_half), BF16),
             pltpu.VMEM(ids.shape, jnp.int32),
             dma((1,)), dma((4,)), dma((8,)), dma((1,)),
             dma((4,)), dma((4,)), dma((8,)), dma((8,)), dma((4,)), dma((4,)),
-            dma((4,)), dma((4,)),
-            dma((4,)), dma((4,)), dma((8,)), dma((8,)), dma((4,)), dma((4,)),
+            dma((8,)), dma((8,)),
+            dma((8,)), dma((8,)), dma((16,)), dma((16,)), dma((8,)), dma((8,)),
             dma((16,)), dma((16,)),
         ],
         compiler_params=pltpu.CompilerParams(

time: 43.4 us -> 39.5 us (0.910)
  Pallas kernels: 43.2 us -> 39.4 us
    pallas_call x1, Pallas kernels: 40.3 us -> 36.4 us  [grouped(): pl.pallas_call(expert_kernel, out_shape=jax.ShapeDtypeStruct((16, 16, wid...]
where the time goes in v4:
time: 39.5 us; the launch traced here: 39.4 us
  Pallas kernels  39.4 us (100%)
    pallas_call x1, Pallas kernels, grouped(): pl.pallas_call(expert_kernel, out_shape=jax.ShapeDtypeStruct((16, 16, wid...  36.4 us
    pallas_call x1, Pallas kernels, grouped(): pl.pallas_call(functools.partial(combine_kernel, width), out_shape=jax.Sh...  2.97 us

profile of v4, /device:TPU:0, one launch (start us, length us, event | category | flops | bytes accessed | tf_op | source)
XLA Modules:
  0.0 39.4 jit_solution(3711018542097091927)
XLA Ops:
  0.0 36.4 %shard_map.64.ret_ref = bf16[16,16,256]{2,1,0:T(8,128)(2,1)} custom-call(s32[8,128]{1,0:T(8,128)} %bitcast.4, bf16[128,7168]{1,0:T(8,128)(2,1)} %x_hbm.1, bf16[1792,512]{1,0:T(8,128)(2,1)} %gate_hbm.1, bf16[1792,512]{1,0:T(8,128)(2,1)} %up_hbm.1, bf16[448,2048]{1,0:T(8,128)(2,1)} %bitcast.3), custom_call_target="tpu_custom_call" | custom-call | tf_op jit(solution)/shard_map/pallas_call | solution.py:311
  36.4 3.0 %shard_map.65 = bf16[128,7168]{1,0:T(8,128)(2,1)} custom-call(s32[8,128]{1,0:T(8,128)} %bitcast.5, f32[8,128]{1,0:T(8,128)} %bitcast.6, bf16[16,16,256]{2,1,0:T(8,128)(2,1)} %shard_map.64.ret_ref), custom_call_target="tpu_custom_call" | custom-call | tf_op jit(solution)/shard_map/pallas_call | solution.py:341

commit v5 on v4

--- a/solution.py
+++ b/solution.py
@@ -12,6 +12,8 @@
 MESH = pl.DeviceIdType.MESH
 F32 = jnp.float32
 BF16 = jnp.bfloat16
+BOTH_ROWS = False
+BOTH_HIDDEN = True
 
 
 def slot_rows(ids):
@@ -52,7 +54,7 @@
         return lax.rem(w + 4 - k, 4)
 
     barrier = pltpu.get_barrier_semaphore()
-    for device in [{"wide": ahead(k)} for k in (2, 1, 3)] + [{"narrow": across}, {"narrow": mate}]:
+    for device in [{"wide": ahead(k)} for k in (2, 1, 3)] + [{"narrow": m} for m in (across, diag, mate)]:
         pl.semaphore_signal(barrier, inc=1, device_id=device, device_id_type=MESH)
 
     load_ids = pltpu.make_async_copy(ids_hbm, ids_v, ids_sem.at[0])
@@ -86,7 +88,7 @@
         second = jnp.dot(pick, x_v[k, :, half:], preferred_element_type=F32)
         return jnp.concatenate([first[:CAP], second[CAP:]], axis=0).astype(BF16)
 
-    pl.semaphore_wait(barrier, 5)
+    pl.semaphore_wait(barrier, 6)
 
     def remote(src, dst, send, recv, device):
         return pltpu.make_async_remote_copy(
@@ -101,59 +103,70 @@
         return copy
 
     class Spread:
-        def __init__(self, buf, place, bs, br, cs, cr, base):
-            self.buf, self.place, self.base = buf, place, base
-            self.sems = bs, br, cs, cr
-            self.cross, self.close, self.last = {}, {}, {}
+        def __init__(self, buf, place, sems, base, both):
+            self.buf, self.place, self.base, self.both = buf, place, base, both
+            self.a_s, self.a_r, self.b_s, self.b_r, self.c_s, self.c_r = sems
+            self.mine = buf.at[place(w, n)]
+            self.near, self.cross, self.close, self.far = {}, {}, {}, {}
+
+        def send_near(self, k, source):
+            i = 2 * (self.base + k)
+            self.near[k] = go(remote(source, self.mine, self.a_s.at[i], self.a_r.at[i], {"wide": ahead(k)}))
+
+        def send_cross(self, k, source):
+            if self.both:
+                i = 2 * (self.base + k) + 1
+                device = {"wide": ahead(k), "narrow": across}
+                self.cross[k] = go(remote(source, self.mine, self.a_s.at[i], self.a_r.at[i], device))
 
         def forward(self, k):
-            bs, br, _, _ = self.sems
-            block_ref = self.buf.at[self.place(behind(k), n)]
+            if k:
+                self.near[k].wait_recv()
             i = self.base + k
-            self.cross[k] = go(remote(block_ref, block_ref, bs.at[2 * i], br.at[2 * i], {"narrow": across}))
-            self.close[k] = go(remote(block_ref, block_ref, bs.at[2 * i + 1], br.at[2 * i + 1], {"narrow": mate}))
-
-        def relay(self, k):
-            _, _, cs, cr = self.sems
-            self.cross[k].wait_recv()
-            block_ref = self.buf.at[self.place(behind(k), across)]
-            i = self.base + k
-            self.last[k] = go(remote(block_ref, block_ref, cs.at[i], cr.at[i], {"narrow": mate}))
+            ref = self.buf.at[self.place(behind(k), n)]
+            if not self.both:
+                self.cross[k] = go(remote(ref, ref, self.b_s.at[2 * i], self.b_r.at[2 * i], {"narrow": across}))
+                self.far[k] = go(remote(ref, ref, self.c_s.at[i], self.c_r.at[i], {"narrow": diag}))
+            self.close[k] = go(remote(ref, ref, self.b_s.at[2 * i + 1], self.b_r.at[2 * i + 1], {"narrow": mate}))
+
+        def forward_cross(self, k):
+            if self.both:
+                self.cross[k].wait_recv()
+                i = self.base + k
+                ref = self.buf.at[self.place(behind(k), across)]
+                self.far[k] = go(remote(ref, ref, self.c_s.at[i], self.c_r.at[i], {"narrow": mate}))
 
         def wait_close(self):
             for k in self.close:
                 self.close[k].wait_recv()
 
-        def wait_last(self):
-            for k in self.last:
-                self.last[k].wait_recv()
+        def wait_cross(self):
+            if not self.both:
+                for k in self.cross:
+                    self.cross[k].wait_recv()
+
+        def wait_far(self):
+            for k in self.far:
+                self.far[k].wait_recv()
 
     def seg_place(w_, n_):
         return (n_ // 2) * 8 + w_ * 2 + lax.rem(n_, 2)
 
     seg_mine = seg_place(w, n)
-    a_copies = {}
+    spread = Spread(seg, seg_place, (a_send, a_recv, b_send, b_recv, c_send, c_recv), 0, BOTH_ROWS)
     for i, k in enumerate((2, 1, 3, 0)):
         loads_x[i].wait()
         value = gathered(k)
         if k:
             xq[k] = value
-            a_copies[k] = go(
-                remote(xq.at[k], seg.at[seg_mine], a_send.at[k], a_recv.at[k], {"wide": ahead(k)})
-            )
+            spread.send_near(k, xq.at[k])
         else:
             seg[seg_mine] = value
-    spread = Spread(seg, seg_place, b_send, b_recv, c_send, c_recv, 0)
-    spread.forward(0)
-    a_copies[1].wait_recv()
-    spread.forward(1)
-    spread.relay(0)
-    a_copies[3].wait_recv()
-    spread.forward(3)
-    spread.relay(1)
-    a_copies[2].wait_recv()
-    spread.forward(2)
-    spread.relay(3)
+    for k in (2, 1, 3):
+        spread.send_cross(k, xq.at[k])
+    spread.send_cross(0, seg.at[seg_mine])
+    for k in (0, 1, 3, 2):
+        spread.forward(k)
     spread.wait_close()
 
     side = n // 2
@@ -183,14 +196,15 @@
     partial_sums(0, 2)
     partial_sums(0, 1)
     partial_sums(0, 3)
-    spread.relay(2)
     partial_sums(0, 0)
-    spread.wait_last()
+    for k in (0, 1, 3, 2):
+        spread.forward_cross(k)
+    spread.wait_cross()
+    spread.wait_far()
     fill(1)
     for k in (2, 1, 3, 0):
         partial_sums(1, k)
 
-    h_copies = {}
     h_spread = {}
 
     def hid_place(c):
@@ -210,25 +224,19 @@
         place = hid_place(c)
         mine = place(w, n)
         hid[mine] = (gate / (1.0 + jnp.exp(-gate)) * up).astype(BF16)
+        h_spread[c] = Spread(
+            hid, place, (ha_send, ha_recv, hb_send, hb_recv, hc_send, hc_recv), 4 * c, BOTH_HIDDEN
+        )
         for k in (2, 1, 3):
-            i = 4 * c + k
-            h_copies[i] = go(
-                remote(hid.at[mine], hid.at[mine], ha_send.at[i], ha_recv.at[i], {"wide": ahead(k)})
-            )
-        h_spread[c] = Spread(hid, place, hb_send, hb_recv, hc_send, hc_recv, 4 * c)
+            h_spread[c].send_near(k, hid.at[mine])
+        for k in (2, 1, 3, 0):
+            h_spread[c].send_cross(k, hid.at[mine])
         h_spread[c].forward(0)
-    late = []
     for c in range(2):
-        for done, k in ((0, 1), (1, 3), (3, 2)):
-            h_copies[4 * c + k].wait_recv()
+        for k in (1, 3, 2):
             h_spread[c].forward(k)
-            late.append((c, done))
-            if len(late) > 1:
-                before_c, before_k = late.pop(0)
-                h_spread[before_c].relay(before_k)
-        late.append((c, 2))
-    for before_c, before_k in late:
-        h_spread[before_c].relay(before_k)
+        for k in (0, 1, 3, 2):
+            h_spread[c].forward_cross(k)
     load_down.wait()
 
     def down_part(n_):
@@ -243,12 +251,14 @@
         return lax.dot_general(left, right, (((1,), (1,)), ((), ())), preferred_element_type=F32)
 
     out = down_part(n)
-    out = out + down_part(across)
     for c in range(2):
         h_spread[c].wait_close()
     out = out + down_part(mate)
     for c in range(2):
-        h_spread[c].wait_last()
+        h_spread[c].wait_cross()
+    out = out + down_part(across)
+    for c in range(2):
+        h_spread[c].wait_far()
     out = out + down_part(diag)
 
     width = out.shape[1]
@@ -328,9 +338,9 @@
             pltpu.VMEM((16, 16, wide_half), BF16),
             pltpu.VMEM(ids.shape, jnp.int32),
             dma((1,)), dma((4,)), dma((8,)), dma((1,)),
-            dma((4,)), dma((4,)), dma((8,)), dma((8,)), dma((4,)), dma((4,)),
+            dma((8,)), dma((8,)), dma((8,)), dma((8,)), dma((4,)), dma((4,)),
             dma((8,)), dma((8,)),
-            dma((8,)), dma((8,)), dma((16,)), dma((16,)), dma((8,)), dma((8,)),
+            dma((16,)), dma((16,)), dma((16,)), dma((16,)), dma((8,)), dma((8,)),
             dma((16,)), dma((16,)),
         ],
         compiler_params=pltpu.CompilerParams(

time: 39.5 us -> 35.8 us (0.906)
  Pallas kernels: 39.4 us -> 35.7 us
    pallas_call x1, Pallas kernels: 36.4 us -> 32.7 us  [grouped(): pl.pallas_call(expert_kernel, out_shape=jax.ShapeDtypeStruct((16, 16, wid...]
where the time goes in v5:
time: 35.8 us; the launch traced here: 35.7 us
  Pallas kernels  35.7 us (100%)
    pallas_call x1, Pallas kernels, grouped(): pl.pallas_call(expert_kernel, out_shape=jax.ShapeDtypeStruct((16, 16, wid...  32.7 us
    pallas_call x1, Pallas kernels, grouped(): pl.pallas_call(functools.partial(combine_kernel, width), out_shape=jax.Sh...  2.97 us

profile of v5, /device:TPU:0, one launch (start us, length us, event | category | flops | bytes accessed | tf_op | source)
XLA Modules:
  0.0 35.7 jit_solution(11167156858662177834)
XLA Ops:
  0.0 32.7 %shard_map.64.ret_ref = bf16[16,16,256]{2,1,0:T(8,128)(2,1)} custom-call(s32[8,128]{1,0:T(8,128)} %bitcast.4, bf16[128,7168]{1,0:T(8,128)(2,1)} %x_hbm.1, bf16[1792,512]{1,0:T(8,128)(2,1)} %gate_hbm.1, bf16[1792,512]{1,0:T(8,128)(2,1)} %up_hbm.1, bf16[448,2048]{1,0:T(8,128)(2,1)} %bitcast.3), custom_call_target="tpu_custom_call" | custom-call | tf_op jit(solution)/shard_map/pallas_call | solution.py:321
  32.7 3.0 %shard_map.65 = bf16[128,7168]{1,0:T(8,128)(2,1)} custom-call(s32[8,128]{1,0:T(8,128)} %bitcast.5, f32[8,128]{1,0:T(8,128)} %bitcast.6, bf16[16,16,256]{2,1,0:T(8,128)(2,1)} %shard_map.64.ret_ref), custom_call_target="tpu_custom_call" | custom-call | tf_op jit(solution)/shard_map/pallas_call | solution.py:351

commit v6 on v5

--- a/solution.py
+++ b/solution.py
@@ -320,7 +320,7 @@
     vmem_spec = pl.BlockSpec(memory_space=pltpu.VMEM)
     returned = pl.pallas_call(
         expert_kernel,
-        out_shape=jax.ShapeDtypeStruct((16, 16, wide_half), BF16),
+        out_shape=pltpu.VMEM((16, 16, wide_half), BF16),
         in_specs=[any_spec] * 5,
         out_specs=vmem_spec,
         scratch_shapes=[
@@ -355,7 +355,7 @@
         in_specs=[
             pl.BlockSpec(ids.shape, lambda i: (0, 0)),
             pl.BlockSpec(weights.shape, lambda i: (0, 0)),
-            pl.BlockSpec((16 // parts, 16, wide_half), lambda i: (i, 0, 0)),
+            pl.BlockSpec(memory_space=pltpu.VMEM),
         ],
         out_specs=pl.BlockSpec((rows, model // parts), lambda i: (0, i)),
     )(ids, weights, returned)

time: 35.8 us -> 35.8 us (level)
  Pallas kernels: 35.7 us -> 35 us
  local copies, waits for them, and re-layouts: 0 us -> 0.64 us
    unnamed x0 -> x2, local copies, waits for them, and re-layouts: none -> 0.64 us
    pallas_call x1, Pallas kernels: 32.7 us -> 32.1 us  [grouped(): pl.pallas_call(expert_kernel, out_shape=pltpu.VMEM((16, 16, wide_half), B...]
where the time goes in v6:
time: 35.8 us; the launch traced here: 35.7 us
  Pallas kernels  35 us (98%)
  local copies, waits for them, and re-layouts  0.64 us (2%)
    pallas_call x1, Pallas kernels, grouped(): pl.pallas_call(expert_kernel, out_shape=pltpu.VMEM((16, 16, wide_half), B...  32.1 us
    pallas_call x1, Pallas kernels, grouped(): pl.pallas_call(functools.partial(combine_kernel, width), out_shape=jax.Sh...  2.97 us

profile of v6, /device:TPU:0, one launch (start us, length us, event | category | flops | bytes accessed | tf_op | source)
XLA Modules:
  0.0 35.7 jit_solution(150526664563047029)
XLA Ops:
  0.0 32.1 %shard_map.64.ret_ref = bf16[16,16,256]{2,1,0:T(8,128)(2,1)S(1)} custom-call(s32[8,128]{1,0:T(8,128)} %bitcast.4, bf16[128,7168]{1,0:T(8,128)(2,1)} %x_hbm.1, bf16[1792,512]{1,0:T(8,128)(2,1)} %gate_hbm.1, bf16[1792,512]{1,0:T(8,128)(2,1)} %up_hbm.1, bf16[448,2048]{1,0:T(8,128)(2,1)} %bitcast.3), custom_call_target="tpu_custom_call" | custom-call | tf_op jit(solution)/shard_map/pallas_call | solution.py:321
  32.1 0.0 copy-start
  32.1 0.6 %copy-done = bf16[16,16,256]{2,1,0:T(8,128)(2,1)} copy-done((bf16[16,16,256]{2,1,0:T(8,128)(2,1)}, bf16[16,16,256]{2,1,0:T(8,128)(2,1)S(1)}, u32[]{:S(2)}) %copy-start) | copy-done | bytes 131096
  32.7 3.0 %shard_map.65 = bf16[128,7168]{1,0:T(8,128)(2,1)} custom-call(s32[8,128]{1,0:T(8,128)} %bitcast.5, f32[8,128]{1,0:T(8,128)} %bitcast.6, bf16[16,16,256]{2,1,0:T(8,128)(2,1)} %copy-done), custom_call_target="tpu_custom_call" | custom-call | tf_op jit(solution)/shard_map/pallas_call | solution.py:351
Async XLA Ops:
  32.1 0.7 %copy-start = (bf16[16,16,256]{2,1,0:T(8,128)(2,1)}, bf16[16,16,256]{2,1,0:T(8,128)(2,1)S(1)}, u32[]{:S(2)}) copy-start(bf16[16,16,256]{2,1,0:T(8,128)(2,1)S(1)} %shard_map.64.ret_ref) | copy-start | bytes 393220
